TPU v7x, 128 devices: a whole 4x4x4 slice. The times are simulated.
128 devices in a mesh: cluster: 4 (over z_lo, core), group: 32 (over y, z_hi, x).
Axes of the slice: x: 4, y: 4, z: 4 (z_hi: 2, z_lo: 2; z = z_hi * 2 + z_lo), core: 2. Of those that a mesh axis runs over, the one named last changes fastest.
Arguments:
- embeddings: float32 [49152, 512], P(('cluster', 'group')), may hold values from -220 to 220
- destinations: int32 [49152, 1], P(('cluster', 'group')), may hold values from 0 to 127; in each aligned block of 384 rows (0 to 383, 384 to 767, ...) at most 6 rows name the same one
Outputs:
- nearest: float32 [49152], P(('cluster', 'group'))
Inputs may be any that keep to these rules, and one draw needn't show every extreme that they name: `destinations`: among the rows of one device no destination is named more than 6 times, a bound that some block reaches.
All inputs are finite; a program needn't handle non-finite values.
Results may differ from a plain program's by a relative error of at most 0.005.
Values may be sent and summed in bfloat16 or wider, within the bound.
A program may use at most 64 MiB of HBM per device.

v0:
```python
import jax
import jax.numpy as jnp
from jax import lax
from jax.sharding import PartitionSpec as P


def passed_along(value, axis, steps):
    count = lax.axis_size(axis)
    pairs = [(source, (source + steps) % count) for source in range(count)]
    return lax.ppermute(value, axis, pairs)


def masked_scores(own_rows, own_ids, other_rows, other_ids, same_block):
    scores = lax.dot_general(
        own_rows, other_rows, (((1,), (1,)), ((), ())), preferred_element_type=jnp.float32
    )
    match = (own_ids[:, None] == other_ids[None, :]) & (own_ids[:, None] >= 0)
    if same_block:
        count = own_rows.shape[0]
        match = match & (jnp.arange(count)[:, None] != jnp.arange(count)[None, :])
    return jnp.where(match, scores, jnp.float32(-2.0))


def on_device(embeddings, destinations):
    rows_dev = embeddings.shape[0]
    width = embeddings.shape[1]
    devices = lax.axis_size(("cluster", "group"))
    group_size = lax.axis_size("group")
    capacity = 2 * rows_dev // devices
    slot_count = devices * capacity
    sums = jnp.sum(embeddings * embeddings, axis=1, keepdims=True)
    unit = (embeddings * lax.rsqrt(sums + 1e-06)).astype(jnp.bfloat16)
    target = destinations[:, 0]
    one_hot = (target[:, None] == jnp.arange(devices)[None, :]).astype(jnp.float32)
    earlier = (jnp.arange(rows_dev)[:, None] > jnp.arange(rows_dev)[None, :]).astype(jnp.float32)
    before = jnp.dot(
        earlier, one_hot, precision=lax.Precision.HIGHEST, preferred_element_type=jnp.float32
    )
    rank = jnp.sum(before * one_hot, axis=1).astype(jnp.int32)
    slot = target * capacity + rank
    labels_sent = target // group_size
    send_rows = jnp.zeros((slot_count, width), jnp.bfloat16).at[slot].set(unit)
    send_ids = jnp.full((slot_count,), -1, jnp.int32).at[slot].set(labels_sent)
    own_rows, own_ids = (
        lax.all_to_all(send_rows, ("cluster", "group"), split_axis=0, concat_axis=0, tiled=True),
        lax.all_to_all(send_ids, ("cluster", "group"), split_axis=0, concat_axis=0, tiled=True),
    )
    best = jnp.max(masked_scores(own_rows, own_ids, own_rows, own_ids, True), axis=1)

    def visit(step, carry):
        rows, labels, running = carry
        rows, labels = passed_along((rows, labels), "group", 1)
        scored = masked_scores(own_rows, own_ids, rows, labels, False)
        return (rows, labels, jnp.maximum(running, jnp.max(scored, axis=1)))

    moved_rows, moved_ids, best = lax.fori_loop(1, group_size, visit, (own_rows, own_ids, best))
    back = lax.all_to_all(best, ("cluster", "group"), split_axis=0, concat_axis=0, tiled=True)
    return back[slot]


def solution(mesh):
    in_specs = (P(("cluster", "group"), None), P(("cluster", "group"), None))
    out_specs = P(("cluster", "group"))
    return jax.shard_map(
        on_device, mesh=mesh, in_specs=in_specs, out_specs=out_specs, check_vma=False
    )
```

profile of v0, /device:TPU:1, one launch (start us, length us, event | category | flops | bytes accessed | tf_op | source)
XLA Modules:
  0.0 760.1 jit_solution(13084305397525232317)
XLA Ops:
  33.1 17.7 %all-to-all-done = bf16[128,6,512]{2,1,0:T(8,128)(2,1)S(1)} async-done(((bf16[128,6,512]{2,1,0:T(8,128)(2,1)}), bf16[128,6,512]{2,1,0:T(8,128)(2,1)S(1)}, u32[]{:S(2)}, u32[]{:S(2)}) %all-to-all-start) | async-done | bytes 786464 | tf_op jit(solution)/shard_map/all_to_all | solution.py:45
  52.1 657.6 %while.14 = (s32[]{:T(128)}, bf16[768,512]{1,0:T(8,128)(2,1)S(1)}, s32[768]{0:T(1024)S(1)}, f32[768]{0:T(1024)S(1)}, s32[768]{0:T(1024)S(1)}, /*index=5*/bf16[768,512]{1,0:T(8,128)(2,1)S(1)}, s32[]{:T(128)}) while((s32[]{:T(128)}, bf16[768,512]{1,0:T(8,128)(2,1)S(1)}, s32[768]{0:T(1024)S(1)}, f32[768]{0:T(1024)S(1)}, s32[768]{0:T(1024)S(1)}, ...), condition=%wide.region_7.8_spmd, body=%wide.region_5.7_spmd.sunk | while | flops 606339840 | bytes 6333085 | solution.py:56
  52.9 23.0 %collective-permute-done.1 = s32[768]{0:T(1024)S(1)} collective-permute-done((s32[768]{0:T(1024)S(1)}, s32[768]{0:T(1024)S(1)}, u32[]{:S(2)}, u32[]{:S(2)}) %collective-permute-start.1) | collective-permute-done | bytes 3104 | tf_op jit(solution)/shard_map/while/body/eval_jaxpr/ppermute | solution.py:10
  77.1 22.7 %collective-permute-done.1 = s32[768]{0:T(1024)S(1)} collective-permute-done((s32[768]{0:T(1024)S(1)}, s32[768]{0:T(1024)S(1)}, u32[]{:S(2)}, u32[]{:S(2)}) %collective-permute-start.1) | collective-permute-done | bytes 3104 | tf_op jit(solution)/shard_map/while/body/eval_jaxpr/ppermute | solution.py:10
  100.9 21.7 %collective-permute-done.1 = s32[768]{0:T(1024)S(1)} collective-permute-done((s32[768]{0:T(1024)S(1)}, s32[768]{0:T(1024)S(1)}, u32[]{:S(2)}, u32[]{:S(2)}) %collective-permute-start.1) | collective-permute-done | bytes 3104 | tf_op jit(solution)/shard_map/while/body/eval_jaxpr/ppermute | solution.py:10
  123.8 20.8 %collective-permute-done.1 = s32[768]{0:T(1024)S(1)} collective-permute-done((s32[768]{0:T(1024)S(1)}, s32[768]{0:T(1024)S(1)}, u32[]{:S(2)}, u32[]{:S(2)}) %collective-permute-start.1) | collective-permute-done | bytes 3104 | tf_op jit(solution)/shard_map/while/body/eval_jaxpr/ppermute | solution.py:10
  145.8 19.9 %collective-permute-done.1 = s32[768]{0:T(1024)S(1)} collective-permute-done((s32[768]{0:T(1024)S(1)}, s32[768]{0:T(1024)S(1)}, u32[]{:S(2)}, u32[]{:S(2)}) %collective-permute-start.1) | collective-permute-done | bytes 3104 | tf_op jit(solution)/shard_map/while/body/eval_jaxpr/ppermute | solution.py:10
  166.9 19.0 %collective-permute-done.1 = s32[768]{0:T(1024)S(1)} collective-permute-done((s32[768]{0:T(1024)S(1)}, s32[768]{0:T(1024)S(1)}, u32[]{:S(2)}, u32[]{:S(2)}) %collective-permute-start.1) | collective-permute-done | bytes 3104 | tf_op jit(solution)/shard_map/while/body/eval_jaxpr/ppermute | solution.py:10
  187.1 18.1 %collective-permute-done.1 = s32[768]{0:T(1024)S(1)} collective-permute-done((s32[768]{0:T(1024)S(1)}, s32[768]{0:T(1024)S(1)}, u32[]{:S(2)}, u32[]{:S(2)}) %collective-permute-start.1) | collective-permute-done | bytes 3104 | tf_op jit(solution)/shard_map/while/body/eval_jaxpr/ppermute | solution.py:10
  206.3 17.1 %collective-permute-done.1 = s32[768]{0:T(1024)S(1)} collective-permute-done((s32[768]{0:T(1024)S(1)}, s32[768]{0:T(1024)S(1)}, u32[]{:S(2)}, u32[]{:S(2)}) %collective-permute-start.1) | collective-permute-done | bytes 3104 | tf_op jit(solution)/shard_map/while/body/eval_jaxpr/ppermute | solution.py:10
  224.7 16.5 %collective-permute-done.1 = s32[768]{0:T(1024)S(1)} collective-permute-done((s32[768]{0:T(1024)S(1)}, s32[768]{0:T(1024)S(1)}, u32[]{:S(2)}, u32[]{:S(2)}) %collective-permute-start.1) | collective-permute-done | bytes 3104 | tf_op jit(solution)/shard_map/while/body/eval_jaxpr/ppermute | solution.py:10
  242.3 16.5 %collective-permute-done.1 = s32[768]{0:T(1024)S(1)} collective-permute-done((s32[768]{0:T(1024)S(1)}, s32[768]{0:T(1024)S(1)}, u32[]{:S(2)}, u32[]{:S(2)}) %collective-permute-start.1) | collective-permute-done | bytes 3104 | tf_op jit(solution)/shard_map/while/body/eval_jaxpr/ppermute | solution.py:10
  260.0 17.4 %collective-permute-done.1 = s32[768]{0:T(1024)S(1)} collective-permute-done((s32[768]{0:T(1024)S(1)}, s32[768]{0:T(1024)S(1)}, u32[]{:S(2)}, u32[]{:S(2)}) %collective-permute-start.1) | collective-permute-done | bytes 3104 | tf_op jit(solution)/shard_map/while/body/eval_jaxpr/ppermute | solution.py:10
  278.6 18.5 %collective-permute-done.1 = s32[768]{0:T(1024)S(1)} collective-permute-done((s32[768]{0:T(1024)S(1)}, s32[768]{0:T(1024)S(1)}, u32[]{:S(2)}, u32[]{:S(2)}) %collective-permute-start.1) | collective-permute-done | bytes 3104 | tf_op jit(solution)/shard_map/while/body/eval_jaxpr/ppermute | solution.py:10
  298.3 19.6 %collective-permute-done.1 = s32[768]{0:T(1024)S(1)} collective-permute-done((s32[768]{0:T(1024)S(1)}, s32[768]{0:T(1024)S(1)}, u32[]{:S(2)}, u32[]{:S(2)}) %collective-permute-start.1) | collective-permute-done | bytes 3104 | tf_op jit(solution)/shard_map/while/body/eval_jaxpr/ppermute | solution.py:10
  319.0 20.6 %collective-permute-done.1 = s32[768]{0:T(1024)S(1)} collective-permute-done((s32[768]{0:T(1024)S(1)}, s32[768]{0:T(1024)S(1)}, u32[]{:S(2)}, u32[]{:S(2)}) %collective-permute-start.1) | collective-permute-done | bytes 3104 | tf_op jit(solution)/shard_map/while/body/eval_jaxpr/ppermute | solution.py:10
  340.9 21.7 %collective-permute-done.1 = s32[768]{0:T(1024)S(1)} collective-permute-done((s32[768]{0:T(1024)S(1)}, s32[768]{0:T(1024)S(1)}, u32[]{:S(2)}, u32[]{:S(2)}) %collective-permute-start.1) | collective-permute-done | bytes 3104 | tf_op jit(solution)/shard_map/while/body/eval_jaxpr/ppermute | solution.py:10
  363.8 22.8 %collective-permute-done.1 = s32[768]{0:T(1024)S(1)} collective-permute-done((s32[768]{0:T(1024)S(1)}, s32[768]{0:T(1024)S(1)}, u32[]{:S(2)}, u32[]{:S(2)}) %collective-permute-start.1) | collective-permute-done | bytes 3104 | tf_op jit(solution)/shard_map/while/body/eval_jaxpr/ppermute | solution.py:10
  387.8 23.9 %collective-permute-done.1 = s32[768]{0:T(1024)S(1)} collective-permute-done((s32[768]{0:T(1024)S(1)}, s32[768]{0:T(1024)S(1)}, u32[]{:S(2)}, u32[]{:S(2)}) %collective-permute-start.1) | collective-permute-done | bytes 3104 | tf_op jit(solution)/shard_map/while/body/eval_jaxpr/ppermute | solution.py:10
  412.8 25.2 %collective-permute-done.1 = s32[768]{0:T(1024)S(1)} collective-permute-done((s32[768]{0:T(1024)S(1)}, s32[768]{0:T(1024)S(1)}, u32[]{:S(2)}, u32[]{:S(2)}) %collective-permute-start.1) | collective-permute-done | bytes 3104 | tf_op jit(solution)/shard_map/while/body/eval_jaxpr/ppermute | solution.py:10
  439.2 24.4 %collective-permute-done.1 = s32[768]{0:T(1024)S(1)} collective-permute-done((s32[768]{0:T(1024)S(1)}, s32[768]{0:T(1024)S(1)}, u32[]{:S(2)}, u32[]{:S(2)}) %collective-permute-start.1) | collective-permute-done | bytes 3104 | tf_op jit(solution)/shard_map/while/body/eval_jaxpr/ppermute | solution.py:10
  464.8 23.4 %collective-permute-done.1 = s32[768]{0:T(1024)S(1)} collective-permute-done((s32[768]{0:T(1024)S(1)}, s32[768]{0:T(1024)S(1)}, u32[]{:S(2)}, u32[]{:S(2)}) %collective-permute-start.1) | collective-permute-done | bytes 3104 | tf_op jit(solution)/shard_map/while/body/eval_jaxpr/ppermute | solution.py:10
  489.4 22.5 %collective-permute-done.1 = s32[768]{0:T(1024)S(1)} collective-permute-done((s32[768]{0:T(1024)S(1)}, s32[768]{0:T(1024)S(1)}, u32[]{:S(2)}, u32[]{:S(2)}) %collective-permute-start.1) | collective-permute-done | bytes 3104 | tf_op jit(solution)/shard_map/while/body/eval_jaxpr/ppermute | solution.py:10
  513.1 21.6 %collective-permute-done.1 = s32[768]{0:T(1024)S(1)} collective-permute-done((s32[768]{0:T(1024)S(1)}, s32[768]{0:T(1024)S(1)}, u32[]{:S(2)}, u32[]{:S(2)}) %collective-permute-start.1) | collective-permute-done | bytes 3104 | tf_op jit(solution)/shard_map/while/body/eval_jaxpr/ppermute | solution.py:10
  535.9 20.7 %collective-permute-done.1 = s32[768]{0:T(1024)S(1)} collective-permute-done((s32[768]{0:T(1024)S(1)}, s32[768]{0:T(1024)S(1)}, u32[]{:S(2)}, u32[]{:S(2)}) %collective-permute-start.1) | collective-permute-done | bytes 3104 | tf_op jit(solution)/shard_map/while/body/eval_jaxpr/ppermute | solution.py:10
  557.8 19.7 %collective-permute-done.1 = s32[768]{0:T(1024)S(1)} collective-permute-done((s32[768]{0:T(1024)S(1)}, s32[768]{0:T(1024)S(1)}, u32[]{:S(2)}, u32[]{:S(2)}) %collective-permute-start.1) | collective-permute-done | bytes 3104 | tf_op jit(solution)/shard_map/while/body/eval_jaxpr/ppermute | solution.py:10
  578.7 18.8 %collective-permute-done.1 = s32[768]{0:T(1024)S(1)} collective-permute-done((s32[768]{0:T(1024)S(1)}, s32[768]{0:T(1024)S(1)}, u32[]{:S(2)}, u32[]{:S(2)}) %collective-permute-start.1) | collective-permute-done | bytes 3104 | tf_op jit(solution)/shard_map/while/body/eval_jaxpr/ppermute | solution.py:10
  598.7 17.9 %collective-permute-done.1 = s32[768]{0:T(1024)S(1)} collective-permute-done((s32[768]{0:T(1024)S(1)}, s32[768]{0:T(1024)S(1)}, u32[]{:S(2)}, u32[]{:S(2)}) %collective-permute-start.1) | collective-permute-done | bytes 3104 | tf_op jit(solution)/shard_map/while/body/eval_jaxpr/ppermute | solution.py:10
  617.8 17.0 %collective-permute-done.1 = s32[768]{0:T(1024)S(1)} collective-permute-done((s32[768]{0:T(1024)S(1)}, s32[768]{0:T(1024)S(1)}, u32[]{:S(2)}, u32[]{:S(2)}) %collective-permute-start.1) | collective-permute-done | bytes 3104 | tf_op jit(solution)/shard_map/while/body/eval_jaxpr/ppermute | solution.py:10
  671.3 17.6 %collective-permute-done.1 = s32[768]{0:T(1024)S(1)} collective-permute-done((s32[768]{0:T(1024)S(1)}, s32[768]{0:T(1024)S(1)}, u32[]{:S(2)}, u32[]{:S(2)}) %collective-permute-start.1) | collective-permute-done | bytes 3104 | tf_op jit(solution)/shard_map/while/body/eval_jaxpr/ppermute | solution.py:10
  690.1 18.7 %collective-permute-done.1 = s32[768]{0:T(1024)S(1)} collective-permute-done((s32[768]{0:T(1024)S(1)}, s32[768]{0:T(1024)S(1)}, u32[]{:S(2)}, u32[]{:S(2)}) %collective-permute-start.1) | collective-permute-done | bytes 3104 | tf_op jit(solution)/shard_map/while/body/eval_jaxpr/ppermute | solution.py:10
  710.5 35.4 %all-to-all-start.2 = ((f32[128,6,1]{1,2,0:T(1,128)}), f32[128,6,1]{1,2,0:T(1,128)S(1)}, u32[]{:S(2)}, u32[]{:S(2)}) async-start(f32[128,6,1]{1,2,0:T(1,128)} %bitcast.1), calls=%async_computation.2 | async-start | bytes 131072 | tf_op jit(solution)/shard_map/all_to_all | solution.py:57
  (281 shorter events, 117.7 us)
Async XLA Ops:
  5.4 21.1 %all-to-all-start.1 = ((s32[128,6,1]{1,2,0:T(1,128)}), s32[128,6,1]{1,2,0:T(1,128)S(1)}, u32[]{:S(2)}, u32[]{:S(2)}) async-start(s32[128,6,1]{1,2,0:T(1,128)} %bitcast), calls=%async_computation.1 | async-start | bytes 131072 | tf_op jit(solution)/shard_map/all_to_all | solution.py:46
  26.5 24.3 %all-to-all-start = ((bf16[128,6,512]{2,1,0:T(8,128)(2,1)}), bf16[128,6,512]{2,1,0:T(8,128)(2,1)S(1)}, u32[]{:S(2)}, u32[]{:S(2)}) async-start(bf16[128,6,512]{2,1,0:T(8,128)(2,1)} %all_to_all.24), calls=%async_computation | async-start | bytes 2097152 | tf_op jit(solution)/shard_map/all_to_all | solution.py:45
  52.1 23.8 %collective-permute-start = (bf16[768,512]{1,0:T(8,128)(2,1)S(1)}, bf16[768,512]{1,0:T(8,128)(2,1)S(1)}, u32[]{:S(2)}, u32[]{:S(2)}) collective-permute-start(bf16[768,512]{1,0:T(8,128)(2,1)S(1)} %get-tuple-element.95), channel_id=1, source_target_pairs={{0,1},{1,2},{2,3},{3,4},{4,5},{5,6},{6,7},{7,8},{8,9},{9,10},{10,1... | collective-permute-start | bytes 2359304 | tf_op jit(solution)/shard_map/while/body/eval_jaxpr/ppermute | solution.py:10
  52.5 23.4 %collective-permute-start.1 = (s32[768]{0:T(1024)S(1)}, s32[768]{0:T(1024)S(1)}, u32[]{:S(2)}, u32[]{:S(2)}) collective-permute-start(s32[768]{0:T(1024)S(1)} %get-tuple-element.96), channel_id=1, source_target_pairs={{0,1},{1,2},{2,3},{3,4},{4,5},{5,6},{6,7},{7,8},{8,9},{9,10},{10,1... | collective-permute-start | bytes 9224 | tf_op jit(solution)/shard_map/while/body/eval_jaxpr/ppermute | solution.py:10
  76.9 22.8 %collective-permute-start = (bf16[768,512]{1,0:T(8,128)(2,1)S(1)}, bf16[768,512]{1,0:T(8,128)(2,1)S(1)}, u32[]{:S(2)}, u32[]{:S(2)}) collective-permute-start(bf16[768,512]{1,0:T(8,128)(2,1)S(1)} %get-tuple-element.95), channel_id=1, source_target_pairs={{0,1},{1,2},{2,3},{3,4},{4,5},{5,6},{6,7},{7,8},{8,9},{9,10},{10,1... | collective-permute-start | bytes 2359304 | tf_op jit(solution)/shard_map/while/body/eval_jaxpr/ppermute | solution.py:10
  77.0 22.8 %collective-permute-start.1 = (s32[768]{0:T(1024)S(1)}, s32[768]{0:T(1024)S(1)}, u32[]{:S(2)}, u32[]{:S(2)}) collective-permute-start(s32[768]{0:T(1024)S(1)} %get-tuple-element.96), channel_id=1, source_target_pairs={{0,1},{1,2},{2,3},{3,4},{4,5},{5,6},{6,7},{7,8},{8,9},{9,10},{10,1... | collective-permute-start | bytes 9224 | tf_op jit(solution)/shard_map/while/body/eval_jaxpr/ppermute | solution.py:10
  100.7 21.9 %collective-permute-start = (bf16[768,512]{1,0:T(8,128)(2,1)S(1)}, bf16[768,512]{1,0:T(8,128)(2,1)S(1)}, u32[]{:S(2)}, u32[]{:S(2)}) collective-permute-start(bf16[768,512]{1,0:T(8,128)(2,1)S(1)} %get-tuple-element.95), channel_id=1, source_target_pairs={{0,1},{1,2},{2,3},{3,4},{4,5},{5,6},{6,7},{7,8},{8,9},{9,10},{10,1... | collective-permute-start | bytes 2359304 | tf_op jit(solution)/shard_map/while/body/eval_jaxpr/ppermute | solution.py:10
  100.8 21.8 %collective-permute-start.1 = (s32[768]{0:T(1024)S(1)}, s32[768]{0:T(1024)S(1)}, u32[]{:S(2)}, u32[]{:S(2)}) collective-permute-start(s32[768]{0:T(1024)S(1)} %get-tuple-element.96), channel_id=1, source_target_pairs={{0,1},{1,2},{2,3},{3,4},{4,5},{5,6},{6,7},{7,8},{8,9},{9,10},{10,1... | collective-permute-start | bytes 9224 | tf_op jit(solution)/shard_map/while/body/eval_jaxpr/ppermute | solution.py:10
  123.6 21.0 %collective-permute-start = (bf16[768,512]{1,0:T(8,128)(2,1)S(1)}, bf16[768,512]{1,0:T(8,128)(2,1)S(1)}, u32[]{:S(2)}, u32[]{:S(2)}) collective-permute-start(bf16[768,512]{1,0:T(8,128)(2,1)S(1)} %get-tuple-element.95), channel_id=1, source_target_pairs={{0,1},{1,2},{2,3},{3,4},{4,5},{5,6},{6,7},{7,8},{8,9},{9,10},{10,1... | collective-permute-start | bytes 2359304 | tf_op jit(solution)/shard_map/while/body/eval_jaxpr/ppermute | solution.py:10
  123.7 20.9 %collective-permute-start.1 = (s32[768]{0:T(1024)S(1)}, s32[768]{0:T(1024)S(1)}, u32[]{:S(2)}, u32[]{:S(2)}) collective-permute-start(s32[768]{0:T(1024)S(1)} %get-tuple-element.96), channel_id=1, source_target_pairs={{0,1},{1,2},{2,3},{3,4},{4,5},{5,6},{6,7},{7,8},{8,9},{9,10},{10,1... | collective-permute-start | bytes 9224 | tf_op jit(solution)/shard_map/while/body/eval_jaxpr/ppermute | solution.py:10
  145.6 20.1 %collective-permute-start = (bf16[768,512]{1,0:T(8,128)(2,1)S(1)}, bf16[768,512]{1,0:T(8,128)(2,1)S(1)}, u32[]{:S(2)}, u32[]{:S(2)}) collective-permute-start(bf16[768,512]{1,0:T(8,128)(2,1)S(1)} %get-tuple-element.95), channel_id=1, source_target_pairs={{0,1},{1,2},{2,3},{3,4},{4,5},{5,6},{6,7},{7,8},{8,9},{9,10},{10,1... | collective-permute-start | bytes 2359304 | tf_op jit(solution)/shard_map/while/body/eval_jaxpr/ppermute | solution.py:10
  318.9 20.8 %collective-permute-start = (bf16[768,512]{1,0:T(8,128)(2,1)S(1)}, bf16[768,512]{1,0:T(8,128)(2,1)S(1)}, u32[]{:S(2)}, u32[]{:S(2)}) collective-permute-start(bf16[768,512]{1,0:T(8,128)(2,1)S(1)} %get-tuple-element.95), channel_id=1, source_target_pairs={{0,1},{1,2},{2,3},{3,4},{4,5},{5,6},{6,7},{7,8},{8,9},{9,10},{10,1... | collective-permute-start | bytes 2359304 | tf_op jit(solution)/shard_map/while/body/eval_jaxpr/ppermute | solution.py:10
  318.9 20.7 %collective-permute-start.1 = (s32[768]{0:T(1024)S(1)}, s32[768]{0:T(1024)S(1)}, u32[]{:S(2)}, u32[]{:S(2)}) collective-permute-start(s32[768]{0:T(1024)S(1)} %get-tuple-element.96), channel_id=1, source_target_pairs={{0,1},{1,2},{2,3},{3,4},{4,5},{5,6},{6,7},{7,8},{8,9},{9,10},{10,1... | collective-permute-start | bytes 9224 | tf_op jit(solution)/shard_map/while/body/eval_jaxpr/ppermute | solution.py:10
  340.7 21.9 %collective-permute-start = (bf16[768,512]{1,0:T(8,128)(2,1)S(1)}, bf16[768,512]{1,0:T(8,128)(2,1)S(1)}, u32[]{:S(2)}, u32[]{:S(2)}) collective-permute-start(bf16[768,512]{1,0:T(8,128)(2,1)S(1)} %get-tuple-element.95), channel_id=1, source_target_pairs={{0,1},{1,2},{2,3},{3,4},{4,5},{5,6},{6,7},{7,8},{8,9},{9,10},{10,1... | collective-permute-start | bytes 2359304 | tf_op jit(solution)/shard_map/while/body/eval_jaxpr/ppermute | solution.py:10
  340.8 21.8 %collective-permute-start.1 = (s32[768]{0:T(1024)S(1)}, s32[768]{0:T(1024)S(1)}, u32[]{:S(2)}, u32[]{:S(2)}) collective-permute-start(s32[768]{0:T(1024)S(1)} %get-tuple-element.96), channel_id=1, source_target_pairs={{0,1},{1,2},{2,3},{3,4},{4,5},{5,6},{6,7},{7,8},{8,9},{9,10},{10,1... | collective-permute-start | bytes 9224 | tf_op jit(solution)/shard_map/while/body/eval_jaxpr/ppermute | solution.py:10
  363.6 23.0 %collective-permute-start = (bf16[768,512]{1,0:T(8,128)(2,1)S(1)}, bf16[768,512]{1,0:T(8,128)(2,1)S(1)}, u32[]{:S(2)}, u32[]{:S(2)}) collective-permute-start(bf16[768,512]{1,0:T(8,128)(2,1)S(1)} %get-tuple-element.95), channel_id=1, source_target_pairs={{0,1},{1,2},{2,3},{3,4},{4,5},{5,6},{6,7},{7,8},{8,9},{9,10},{10,1... | collective-permute-start | bytes 2359304 | tf_op jit(solution)/shard_map/while/body/eval_jaxpr/ppermute | solution.py:10
  363.7 22.9 %collective-permute-start.1 = (s32[768]{0:T(1024)S(1)}, s32[768]{0:T(1024)S(1)}, u32[]{:S(2)}, u32[]{:S(2)}) collective-permute-start(s32[768]{0:T(1024)S(1)} %get-tuple-element.96), channel_id=1, source_target_pairs={{0,1},{1,2},{2,3},{3,4},{4,5},{5,6},{6,7},{7,8},{8,9},{9,10},{10,1... | collective-permute-start | bytes 9224 | tf_op jit(solution)/shard_map/while/body/eval_jaxpr/ppermute | solution.py:10
  387.6 24.1 %collective-permute-start = (bf16[768,512]{1,0:T(8,128)(2,1)S(1)}, bf16[768,512]{1,0:T(8,128)(2,1)S(1)}, u32[]{:S(2)}, u32[]{:S(2)}) collective-permute-start(bf16[768,512]{1,0:T(8,128)(2,1)S(1)} %get-tuple-element.95), channel_id=1, source_target_pairs={{0,1},{1,2},{2,3},{3,4},{4,5},{5,6},{6,7},{7,8},{8,9},{9,10},{10,1... | collective-permute-start | bytes 2359304 | tf_op jit(solution)/shard_map/while/body/eval_jaxpr/ppermute | solution.py:10
  387.7 24.0 %collective-permute-start.1 = (s32[768]{0:T(1024)S(1)}, s32[768]{0:T(1024)S(1)}, u32[]{:S(2)}, u32[]{:S(2)}) collective-permute-start(s32[768]{0:T(1024)S(1)} %get-tuple-element.96), channel_id=1, source_target_pairs={{0,1},{1,2},{2,3},{3,4},{4,5},{5,6},{6,7},{7,8},{8,9},{9,10},{10,1... | collective-permute-start | bytes 9224 | tf_op jit(solution)/shard_map/while/body/eval_jaxpr/ppermute | solution.py:10
  412.7 25.4 %collective-permute-start = (bf16[768,512]{1,0:T(8,128)(2,1)S(1)}, bf16[768,512]{1,0:T(8,128)(2,1)S(1)}, u32[]{:S(2)}, u32[]{:S(2)}) collective-permute-start(bf16[768,512]{1,0:T(8,128)(2,1)S(1)} %get-tuple-element.95), channel_id=1, source_target_pairs={{0,1},{1,2},{2,3},{3,4},{4,5},{5,6},{6,7},{7,8},{8,9},{9,10},{10,1... | collective-permute-start | bytes 2359304 | tf_op jit(solution)/shard_map/while/body/eval_jaxpr/ppermute | solution.py:10
  412.7 25.3 %collective-permute-start.1 = (s32[768]{0:T(1024)S(1)}, s32[768]{0:T(1024)S(1)}, u32[]{:S(2)}, u32[]{:S(2)}) collective-permute-start(s32[768]{0:T(1024)S(1)} %get-tuple-element.96), channel_id=1, source_target_pairs={{0,1},{1,2},{2,3},{3,4},{4,5},{5,6},{6,7},{7,8},{8,9},{9,10},{10,1... | collective-permute-start | bytes 9224 | tf_op jit(solution)/shard_map/while/body/eval_jaxpr/ppermute | solution.py:10
  439.1 24.6 %collective-permute-start = (bf16[768,512]{1,0:T(8,128)(2,1)S(1)}, bf16[768,512]{1,0:T(8,128)(2,1)S(1)}, u32[]{:S(2)}, u32[]{:S(2)}) collective-permute-start(bf16[768,512]{1,0:T(8,128)(2,1)S(1)} %get-tuple-element.95), channel_id=1, source_target_pairs={{0,1},{1,2},{2,3},{3,4},{4,5},{5,6},{6,7},{7,8},{8,9},{9,10},{10,1... | collective-permute-start | bytes 2359304 | tf_op jit(solution)/shard_map/while/body/eval_jaxpr/ppermute | solution.py:10
  439.1 24.5 %collective-permute-start.1 = (s32[768]{0:T(1024)S(1)}, s32[768]{0:T(1024)S(1)}, u32[]{:S(2)}, u32[]{:S(2)}) collective-permute-start(s32[768]{0:T(1024)S(1)} %get-tuple-element.96), channel_id=1, source_target_pairs={{0,1},{1,2},{2,3},{3,4},{4,5},{5,6},{6,7},{7,8},{8,9},{9,10},{10,1... | collective-permute-start | bytes 9224 | tf_op jit(solution)/shard_map/while/body/eval_jaxpr/ppermute | solution.py:10
  464.6 23.6 %collective-permute-start = (bf16[768,512]{1,0:T(8,128)(2,1)S(1)}, bf16[768,512]{1,0:T(8,128)(2,1)S(1)}, u32[]{:S(2)}, u32[]{:S(2)}) collective-permute-start(bf16[768,512]{1,0:T(8,128)(2,1)S(1)} %get-tuple-element.95), channel_id=1, source_target_pairs={{0,1},{1,2},{2,3},{3,4},{4,5},{5,6},{6,7},{7,8},{8,9},{9,10},{10,1... | collective-permute-start | bytes 2359304 | tf_op jit(solution)/shard_map/while/body/eval_jaxpr/ppermute | solution.py:10
  464.7 23.5 %collective-permute-start.1 = (s32[768]{0:T(1024)S(1)}, s32[768]{0:T(1024)S(1)}, u32[]{:S(2)}, u32[]{:S(2)}) collective-permute-start(s32[768]{0:T(1024)S(1)} %get-tuple-element.96), channel_id=1, source_target_pairs={{0,1},{1,2},{2,3},{3,4},{4,5},{5,6},{6,7},{7,8},{8,9},{9,10},{10,1... | collective-permute-start | bytes 9224 | tf_op jit(solution)/shard_map/while/body/eval_jaxpr/ppermute | solution.py:10
  489.2 22.7 %collective-permute-start = (bf16[768,512]{1,0:T(8,128)(2,1)S(1)}, bf16[768,512]{1,0:T(8,128)(2,1)S(1)}, u32[]{:S(2)}, u32[]{:S(2)}) collective-permute-start(bf16[768,512]{1,0:T(8,128)(2,1)S(1)} %get-tuple-element.95), channel_id=1, source_target_pairs={{0,1},{1,2},{2,3},{3,4},{4,5},{5,6},{6,7},{7,8},{8,9},{9,10},{10,1... | collective-permute-start | bytes 2359304 | tf_op jit(solution)/shard_map/while/body/eval_jaxpr/ppermute | solution.py:10
  489.3 22.6 %collective-permute-start.1 = (s32[768]{0:T(1024)S(1)}, s32[768]{0:T(1024)S(1)}, u32[]{:S(2)}, u32[]{:S(2)}) collective-permute-start(s32[768]{0:T(1024)S(1)} %get-tuple-element.96), channel_id=1, source_target_pairs={{0,1},{1,2},{2,3},{3,4},{4,5},{5,6},{6,7},{7,8},{8,9},{9,10},{10,1... | collective-permute-start | bytes 9224 | tf_op jit(solution)/shard_map/while/body/eval_jaxpr/ppermute | solution.py:10
  512.9 21.8 %collective-permute-start = (bf16[768,512]{1,0:T(8,128)(2,1)S(1)}, bf16[768,512]{1,0:T(8,128)(2,1)S(1)}, u32[]{:S(2)}, u32[]{:S(2)}) collective-permute-start(bf16[768,512]{1,0:T(8,128)(2,1)S(1)} %get-tuple-element.95), channel_id=1, source_target_pairs={{0,1},{1,2},{2,3},{3,4},{4,5},{5,6},{6,7},{7,8},{8,9},{9,10},{10,1... | collective-permute-start | bytes 2359304 | tf_op jit(solution)/shard_map/while/body/eval_jaxpr/ppermute | solution.py:10
  513.0 21.7 %collective-permute-start.1 = (s32[768]{0:T(1024)S(1)}, s32[768]{0:T(1024)S(1)}, u32[]{:S(2)}, u32[]{:S(2)}) collective-permute-start(s32[768]{0:T(1024)S(1)} %get-tuple-element.96), channel_id=1, source_target_pairs={{0,1},{1,2},{2,3},{3,4},{4,5},{5,6},{6,7},{7,8},{8,9},{9,10},{10,1... | collective-permute-start | bytes 9224 | tf_op jit(solution)/shard_map/while/body/eval_jaxpr/ppermute | solution.py:10
  535.7 20.9 %collective-permute-start = (bf16[768,512]{1,0:T(8,128)(2,1)S(1)}, bf16[768,512]{1,0:T(8,128)(2,1)S(1)}, u32[]{:S(2)}, u32[]{:S(2)}) collective-permute-start(bf16[768,512]{1,0:T(8,128)(2,1)S(1)} %get-tuple-element.95), channel_id=1, source_target_pairs={{0,1},{1,2},{2,3},{3,4},{4,5},{5,6},{6,7},{7,8},{8,9},{9,10},{10,1... | collective-permute-start | bytes 2359304 | tf_op jit(solution)/shard_map/while/body/eval_jaxpr/ppermute | solution.py:10
  535.8 20.8 %collective-permute-start.1 = (s32[768]{0:T(1024)S(1)}, s32[768]{0:T(1024)S(1)}, u32[]{:S(2)}, u32[]{:S(2)}) collective-permute-start(s32[768]{0:T(1024)S(1)} %get-tuple-element.96), channel_id=1, source_target_pairs={{0,1},{1,2},{2,3},{3,4},{4,5},{5,6},{6,7},{7,8},{8,9},{9,10},{10,1... | collective-permute-start | bytes 9224 | tf_op jit(solution)/shard_map/while/body/eval_jaxpr/ppermute | solution.py:10
  710.5 45.1 %all-to-all-start.2 = ((f32[128,6,1]{1,2,0:T(1,128)}), f32[128,6,1]{1,2,0:T(1,128)S(1)}, u32[]{:S(2)}, u32[]{:S(2)}) async-start(f32[128,6,1]{1,2,0:T(1,128)} %bitcast.1), calls=%async_computation.2 | async-start | bytes 131072 | tf_op jit(solution)/shard_map/all_to_all | solution.py:57
  (34 other events, 613.3 us)
where the time goes:
time: 760 us
  waiting for transfers between devices  652 us (86%)
  starting transfers between devices  57.1 us (8%)
  matrix products  29.3 us (4%)
  local copies, waits for them, and re-layouts  12 us (2%)
    ppermute x62, waiting for transfers between devices, passed_along(): return lax.ppermute(value, axis, pairs)  620 us
    all_to_all x1, starting transfers between devices, on_device(): lax.all_to_all(best, ('cluster', 'group'), split_axis=0, concat_axis=0, t...  35.4 us
    dot_general x32, matrix products, masked_scores(): lax.dot_general(own_rows, other_rows, (((1,), (1,)), ((), ())), preferred...  29.1 us
    all_to_all x1, waiting for transfers between devices, on_device(): lax.all_to_all(send_rows, ('cluster', 'group'), split_axis=0, concat_axis...  17.7 us
  transfers between devices with their start and end apart: 65, of which 34 were waited for; matrix products, arithmetic and copies ran while one was open for 1% of the time, Pallas kernels for 0%

commit v1 on v0

v1 whole, which is shorter than its diff:
```python
import functools

import jax
import jax.numpy as jnp
from jax import lax
from jax.experimental import pallas as pl
from jax.experimental.pallas import tpu as pltpu
from jax.sharding import PartitionSpec as P

MESH = pl.DeviceIdType.MESH
HALF = 384
WIDTH = 512
TILE = 16
UNITS = ((1, 0, 0), (3, 0, 0), (0, 1, 0), (0, 3, 0), (0, 0, 1), (0, 0, 3))
SLOTS = 13
OFFSETS = ((0, 0, 0), (0, 1, 0), (0, 3, 1), (0, 0, 3), (1, 0, 0), (0, 2, 1), (0, 3, 0), (2, 0, 0), (3, 0, 3), (2, 0, 3), (0, 2, 0), (0, 0, 1), (0, 1, 1))
PARTS = ((0, 128), (128, 128), (256, 144))
ACTS = (
    ("D", 0), ("S", 0, 4, 0, 0), ("S", 0, 1, 1, 2), ("S", 0, 6, 1, 3), ("S", 0, 11, 0, 4), ("S", 0, 3, 2, 5),
    ("S", 0, 4, 1, 0), ("S", 0, 1, 2, 2), ("S", 0, 6, 2, 3), ("S", 0, 11, 2, 4), ("S", 0, 3, 1, 5), ("self", 0),
    ("X", 0), ("self", 1), ("S", 0, 4, 2, 0), ("S", 0, 1, 0, 2), ("S", 0, 3, 0, 5), ("S", 0, 11, 1, 4), ("R", 4, 0),
    ("S", 4, 7, 0, 0), ("R", 1, 1), ("R", 6, 1), ("S", 6, 2, 1, 4), ("R", 11, 0), ("S", 11, 2, 0, 3), ("R", 3, 2),
    ("S", 3, 8, 2, 1), ("S", 11, 12, 0, 2), ("S", 1, 12, 1, 4), ("R", 4, 1), ("S", 4, 7, 1, 0), ("R", 1, 2),
    ("R", 6, 2), ("R", 11, 2), ("S", 11, 12, 2, 2), ("S", 11, 2, 2, 3), ("R", 3, 1), ("S", 3, 8, 1, 1), ("R", 8, 2),
    ("R", 4, 2), ("S", 4, 7, 2, 0), ("D", 4), ("R", 1, 0), ("D", 1), ("R", 2, 0), ("S", 2, 5, 0, 3),
    ("S", 2, 6, 0, 5), ("R", 11, 1), ("D", 11), ("R", 3, 0), ("S", 3, 8, 0, 1), ("D", 3), ("G", 4, (0,)),
    ("G", 1, (0,)), ("G", 3, (0,)), ("S", 8, 9, 2, 1), ("S", 1, 10, 2, 2), ("S", 6, 10, 1, 3), ("X", 4),
    ("G", 11, (4,)), ("R", 8, 1), ("S", 8, 9, 1, 1), ("X", 3), ("X", 1), ("G", 4, (3, 1)), ("R", 7, 0),
    ("S", 7, 9, 0, 5), ("R", 12, 0), ("R", 2, 2), ("R", 2, 1), ("S", 2, 5, 1, 3), ("D", 2), ("G", 2, (0, 4)),
    ("G", 2, (1, 3)), ("R", 6, 0), ("D", 6), ("R", 8, 0), ("D", 8), ("G", 8, (4, 1)), ("R", 7, 1), ("R", 12, 2),
    ("S", 12, 5, 2, 2), ("R", 5, 0), ("S", 5, 10, 0, 5), ("R", 12, 1), ("D", 12), ("X", 2), ("X", 11),
    ("G", 8, (2, 11)), ("G", 6, (1, 4)), ("R", 9, 2), ("X", 8), ("G", 12, (4, 8)), ("R", 9, 0), ("R", 7, 2),
    ("D", 7), ("R", 10, 2), ("R", 10, 1), ("G", 7, (0, 1)), ("F", 0), ("X", 12), ("G", 7, (2, 12)), ("F", 12),
    ("R", 9, 1), ("G", 9, (2, 11)), ("F", 2), ("R", 10, 0), ("R", 5, 2), ("R", 5, 1), ("D", 5), ("G", 5, (4, 3)),
    ("G", 10, (4, 8)), ("F", 4), ("G", 3, (1,)), ("F", 1), ("G", 11, (3,)), ("F", 3), ("F", 11), ("X", 6),
    ("G", 8, (6,)), ("F", 6), ("G", 5, (8,)), ("F", 8), ("X", 5), ("G", 7, (5,)), ("G", 9, (5,)), ("F", 9),
    ("F", 5), ("X", 7), ("G", 10, (7,)), ("F", 10), ("F", 7),
)


def place():
    cluster = lax.axis_index("cluster")
    group = lax.axis_index("group")
    core = lax.rem(cluster, 2)
    z = cluster // 2 + 2 * lax.rem(group // 4, 2)
    return (lax.rem(group, 4), group // 8, z), core


def device(chip, offset, core):
    x, y, z = (lax.rem(a + b, 4) for a, b in zip(chip, offset))
    return (lax.rem(z, 2) * 2 + core, (y * 2 + z // 2) * 4 + x)


def back(offset):
    return tuple((4 - v) % 4 for v in offset)


def kernel(emb_ref, dest_ref, out_ref, blk, labc, racc, cacc, res,
           ici_send, ici_recv, d2d_send, d2d_recv, res_send, res_recv):
    chip, core = place()
    other = 1 - core
    barrier = pltpu.get_barrier_semaphore()
    for unit in UNITS:
        pl.semaphore_signal(barrier, inc=1, device_id=device(chip, unit, core), device_id_type=MESH)
    sibling = device(chip, (0, 0, 0), other)
    pl.semaphore_signal(barrier, inc=1, device_id=sibling, device_id_type=MESH)

    values = emb_ref[...]
    sums = jnp.sum(values * values, axis=1, keepdims=True)
    blk[0, core, 0:HALF, :] = (values * lax.rsqrt(sums + 1e-06)).astype(jnp.bfloat16)
    label = (dest_ref[...] // 32).astype(jnp.float32)
    tile = jnp.concatenate(
        [jnp.broadcast_to(label, (TILE, HALF)), jnp.zeros((TILE, WIDTH - HALF), jnp.float32)], axis=1)
    blk[0, core, HALF:HALF + TILE, :] = tile.astype(jnp.bfloat16)
    pl.semaphore_wait(barrier, len(UNITS) + 1)

    sends = []

    def ici(src, dst, part, e):
        first, count = PARTS[part]
        rows = pl.ds(first, count)
        return pltpu.make_async_remote_copy(
            src_ref=blk.at[src, core, rows], dst_ref=blk.at[dst, core, rows],
            send_sem=ici_send.at[dst, part], recv_sem=ici_recv.at[dst, part],
            device_id=device(chip, back(UNITS[e]), core), device_id_type=MESH)

    def d2d(slot, half):
        return pltpu.make_async_remote_copy(
            src_ref=blk.at[slot, half], dst_ref=blk.at[slot, half],
            send_sem=d2d_send.at[slot], recv_sem=d2d_recv.at[slot],
            device_id=sibling, device_id_type=MESH)

    def result(slot, half, sender):
        return pltpu.make_async_remote_copy(
            src_ref=cacc.at[slot, half], dst_ref=res.at[slot, sender],
            send_sem=res_send.at[slot, half], recv_sem=res_recv.at[slot, sender],
            device_id=device(chip, OFFSETS[slot], half), device_id_type=MESH)

    def labels(slot, half):
        return blk[slot, half, HALF:HALF + TILE, :].astype(jnp.float32)[0:8, 0:HALF]

    def column_labels(slot):
        row = labels(slot, core)
        labc[slot] = jnp.concatenate([row] * 16, axis=0).T

    have_labc, have_racc, have_cacc = set(), set(), set()

    def prepare(slot):
        if slot not in have_labc:
            have_labc.add(slot)
            column_labels(slot)

    def masked(scores, own, row):
        count = scores.shape[0] // 8
        match = own.reshape(count, 8, 128) == row[None]
        return jnp.where(match, scores.reshape(count, 8, 128), jnp.float32(-2.0))

    def dot(lhs, rhs):
        return lax.dot_general(lhs, rhs, (((1,), (1,)), ((), ())), preferred_element_type=jnp.float32)

    def own_block(which):
        prepare(0)
        half = core if which == 0 else other
        scores = dot(blk[0, core, 0:HALF, :], blk[0, half, 0:HALF, :])
        row = labels(0, half)
        own = labc[0]
        best = racc[0] if 0 in have_racc else jnp.full((HALF, 128), -2.0, jnp.float32)
        for q in range(0, HALF, 128):
            t = masked(scores[:, q:q + 128], own, row[:, q:q + 128]).reshape(HALF, 128)
            if which == 0:
                i = lax.broadcasted_iota(jnp.int32, (HALF, 128), 0)
                j = lax.broadcasted_iota(jnp.int32, (HALF, 128), 1) + q
                t = jnp.where(i == j, jnp.float32(-2.0), t)
            best = jnp.maximum(best, t)
        racc[0] = best
        have_racc.add(0)

    def pairs(slot, others):
        prepare(slot)
        lhs = blk[slot, core, 0:HALF, :]
        own = labc[slot]
        best = racc[slot] if slot in have_racc else None
        for mate in others:
            scores = dot(lhs, blk[mate, :, 0:HALF, :].reshape(2 * HALF, WIDTH))
            for half in range(2):
                row = labels(mate, half)
                for q in range(0, HALF, 128):
                    at = half * HALF + q
                    t = masked(scores[:, at:at + 128], own, row[:, q:q + 128])
                    top = jnp.max(t, axis=0)
                    if mate in have_cacc:
                        top = jnp.maximum(top, cacc[mate, half, :, q:q + 128])
                    cacc[mate, half, :, q:q + 128] = top
                    t = t.reshape(HALF, 128)
                    best = t if best is None else jnp.maximum(best, t)
            have_cacc.add(mate)
        racc[slot] = best
        have_racc.add(slot)

    def finish(slot):
        if slot in have_racc:
            best = jnp.max(racc[slot].T.reshape(16, 8, HALF), axis=0)
            if slot in have_cacc:
                best = jnp.maximum(best, cacc[slot, core])
            cacc[slot, core] = best
        if slot == 0:
            copy = result(0, other, 1)
            copy.start()
            sends.append(copy)
        elif slot in have_cacc:
            for half in range(2):
                copy = result(slot, half, core)
                copy.start()
                sends.append(copy)
        else:
            copy = result(slot, core, core)
            copy.start()
            sends.append(copy)

    for act in ACTS:
        kind = act[0]
        if kind == "S":
            copy = ici(act[1], act[2], act[3], act[4])
            copy.start()
            sends.append(copy)
        elif kind == "R":
            ici(act[1], act[1], act[2], 0).wait_recv()
        elif kind == "D":
            copy = d2d(act[1], core)
            copy.start()
            sends.append(copy)
        elif kind == "X":
            d2d(act[1], other).wait_recv()
        elif kind == "self":
            own_block(act[1])
        elif kind == "G":
            pairs(act[1], act[2])
        else:
            finish(act[1])

    result(0, other, 1).wait_recv()
    best = jnp.maximum(cacc[0, core], res[0, 1])
    for slot in range(1, SLOTS):
        if slot in have_cacc:
            for sender in range(2):
                result(slot, core, sender).wait_recv()
                best = jnp.maximum(best, res[slot, sender])
        else:
            result(slot, core, core).wait_recv()
            best = jnp.maximum(best, res[slot, core])
    out_ref[...] = jnp.max(best, axis=0, keepdims=True)
    for copy in sends:
        copy.wait_send()


def on_device(embeddings, destinations):
    nearest = pl.pallas_call(
        kernel,
        out_shape=jax.ShapeDtypeStruct((1, HALF), jnp.float32),
        in_specs=[pl.BlockSpec(memory_space=pltpu.VMEM)] * 2,
        out_specs=pl.BlockSpec(memory_space=pltpu.VMEM),
        scratch_shapes=[
            pltpu.VMEM((SLOTS, 2, HALF + TILE, WIDTH), jnp.bfloat16),
            pltpu.VMEM((SLOTS, HALF, 128), jnp.float32),
            pltpu.VMEM((SLOTS, HALF, 128), jnp.float32),
            pltpu.VMEM((SLOTS, 2, 8, HALF), jnp.float32),
            pltpu.VMEM((SLOTS, 2, 8, HALF), jnp.float32),
            pltpu.SemaphoreType.DMA((SLOTS, len(PARTS))),
            pltpu.SemaphoreType.DMA((SLOTS, len(PARTS))),
            pltpu.SemaphoreType.DMA((SLOTS,)),
            pltpu.SemaphoreType.DMA((SLOTS,)),
            pltpu.SemaphoreType.DMA((SLOTS, 2)),
            pltpu.SemaphoreType.DMA((SLOTS, 2)),
        ],
        compiler_params=pltpu.CompilerParams(
            collective_id=0, has_side_effects=True, vmem_limit_bytes=48 * 2**20),
    )(embeddings, destinations.reshape(1, HALF))
    return nearest.reshape(HALF)


def solution(mesh):
    spec = P(("cluster", "group"), None)
    return jax.shard_map(
        on_device, mesh=mesh, in_specs=(spec, spec), out_specs=P(("cluster", "group")), check_vma=False
    )
```

time: 760 us -> 45.6 us (0.06)
  waiting for transfers between devices: 652 us -> 0 us
  starting transfers between devices: 57.1 us -> 0 us
  Pallas kernels: 0 us -> 43.1 us
  matrix products: 29.3 us -> 0 us
  local copies, waits for them, and re-layouts: 12 us -> 1.81 us
    ppermute x62 -> x0, waiting for transfers between devices: 620 us -> none  [passed_along(): return lax.ppermute(value, axis, pairs)]
    all_to_all x3 -> x0, starting transfers between devices: 51.9 us -> none  [the longest x1 35.4 us: on_device(): lax.all_to_all(best, ('cluster', 'group'), split_axis=0, concat_axis=0, t...]
    pallas_call x0 -> x1, Pallas kernels: none -> 43.1 us  [on_device(): pl.pallas_call(kernel, out_shape=jax.ShapeDtypeStruct((1, HALF), jnp.floa...]
    all_to_all x3 -> x0, waiting for transfers between devices: 32.1 us -> none  [the longest x1 17.7 us: on_device(): lax.all_to_all(send_rows, ('cluster', 'group'), split_axis=0, concat_axis...]
    dot_general x33 -> x0, matrix products: 29.3 us -> none  [the longest x32 29.1 us: masked_scores(): lax.dot_general(own_rows, other_rows, (((1,), (1,)), ((), ())), preferred...]
  transfers between devices with their start and end apart: 65 -> 0, of which waited for: 34 -> 0; matrix products, arithmetic and copies ran while one was open for 1% -> 0% of each run, Pallas kernels for 0% -> 0%
where the time goes in v1:
time: 45.6 us; the launch traced here: 45.5 us
  Pallas kernels  43.1 us (95%)
  local copies, waits for them, and re-layouts  1.81 us (4%)
  other arithmetic  0.6 us (1%)
    pallas_call x1, Pallas kernels, on_device(): pl.pallas_call(kernel, out_shape=jax.ShapeDtypeStruct((1, HALF), jnp.floa...  43.1 us
    unnamed x4, local copies, waits for them, and re-layouts  1.81 us

profile of v1, /device:TPU:1, one launch (start us, length us, event | category | flops | bytes accessed | tf_op | source)
XLA Modules:
  0.0 45.5 jit_solution(14437161415251286603)
XLA Ops:
  0.0 0.0 copy-start.1
  0.0 0.7 %copy-done.1 = s32[384,1]{0,1:T(1,128)S(1)} copy-done((s32[384,1]{0,1:T(1,128)S(1)}, s32[384,1]{0,1:T(1,128)}, u32[]{:S(2)}) %copy-start.1) | copy-done | bytes 1560
  0.7 0.0 copy-start
  0.7 1.1 %copy-done = f32[384,512]{1,0:T(8,128)S(1)} copy-done((f32[384,512]{1,0:T(8,128)S(1)}, f32[384,512]{1,0:T(8,128)}, u32[]{:S(2)}) %copy-start) | copy-done | bytes 786456
  1.8 43.1 %shard_map.28 = f32[1,384]{1,0:T(1,128)S(1)} custom-call(f32[384,512]{1,0:T(8,128)S(1)} %copy-done, s32[1,384]{1,0:T(1,128)S(1)} %bitcast.1), custom_call_target="tpu_custom_call" | custom-call | tf_op jit(solution)/shard_map/pallas_call | solution.py:217
  44.9 0.6 %reduce = f32[384]{0:T(512)} reduce(f32[1,384]{1,0:T(1,128)S(1)} %shard_map.28, f32[]{:T(128)} %constant), dimensions={0}, to_apply=%pallas_call.3.reduce_sub_computation | reduce | bytes 3076 | tf_op jit(solution)/shard_map/pallas_call | solution.py:217
Async XLA Ops:
  0.0 0.7 %copy-start.1 = (s32[384,1]{0,1:T(1,128)S(1)}, s32[384,1]{0,1:T(1,128)}, u32[]{:S(2)}) copy-start(s32[384,1]{0,1:T(1,128)} %param.3) | copy-start | bytes 4612
  0.7 1.1 %copy-start = (f32[384,512]{1,0:T(8,128)S(1)}, f32[384,512]{1,0:T(8,128)}, u32[]{:S(2)}) copy-start(f32[384,512]{1,0:T(8,128)} %emb_ref.1) | copy-start | bytes 2359300

commit v2 on v1

--- a/solution.py
+++ b/solution.py
@@ -13,28 +13,28 @@
 TILE = 16
 UNITS = ((1, 0, 0), (3, 0, 0), (0, 1, 0), (0, 3, 0), (0, 0, 1), (0, 0, 3))
 SLOTS = 13
-OFFSETS = ((0, 0, 0), (0, 1, 0), (0, 3, 1), (0, 0, 3), (1, 0, 0), (0, 2, 1), (0, 3, 0), (2, 0, 0), (3, 0, 3), (2, 0, 3), (0, 2, 0), (0, 0, 1), (0, 1, 1))
+OFFSETS = ((0, 0, 0), (0, 3, 3), (1, 0, 0), (0, 1, 0), (0, 0, 1), (0, 0, 2), (0, 3, 0), (3, 1, 0), (0, 3, 2), (3, 0, 0), (1, 1, 0), (2, 0, 0), (2, 1, 0))
 PARTS = ((0, 128), (128, 128), (256, 144))
 ACTS = (
-    ("D", 0), ("S", 0, 4, 0, 0), ("S", 0, 1, 1, 2), ("S", 0, 6, 1, 3), ("S", 0, 11, 0, 4), ("S", 0, 3, 2, 5),
-    ("S", 0, 4, 1, 0), ("S", 0, 1, 2, 2), ("S", 0, 6, 2, 3), ("S", 0, 11, 2, 4), ("S", 0, 3, 1, 5), ("self", 0),
-    ("X", 0), ("self", 1), ("S", 0, 4, 2, 0), ("S", 0, 1, 0, 2), ("S", 0, 3, 0, 5), ("S", 0, 11, 1, 4), ("R", 4, 0),
-    ("S", 4, 7, 0, 0), ("R", 1, 1), ("R", 6, 1), ("S", 6, 2, 1, 4), ("R", 11, 0), ("S", 11, 2, 0, 3), ("R", 3, 2),
-    ("S", 3, 8, 2, 1), ("S", 11, 12, 0, 2), ("S", 1, 12, 1, 4), ("R", 4, 1), ("S", 4, 7, 1, 0), ("R", 1, 2),
-    ("R", 6, 2), ("R", 11, 2), ("S", 11, 12, 2, 2), ("S", 11, 2, 2, 3), ("R", 3, 1), ("S", 3, 8, 1, 1), ("R", 8, 2),
-    ("R", 4, 2), ("S", 4, 7, 2, 0), ("D", 4), ("R", 1, 0), ("D", 1), ("R", 2, 0), ("S", 2, 5, 0, 3),
-    ("S", 2, 6, 0, 5), ("R", 11, 1), ("D", 11), ("R", 3, 0), ("S", 3, 8, 0, 1), ("D", 3), ("G", 4, (0,)),
-    ("G", 1, (0,)), ("G", 3, (0,)), ("S", 8, 9, 2, 1), ("S", 1, 10, 2, 2), ("S", 6, 10, 1, 3), ("X", 4),
-    ("G", 11, (4,)), ("R", 8, 1), ("S", 8, 9, 1, 1), ("X", 3), ("X", 1), ("G", 4, (3, 1)), ("R", 7, 0),
-    ("S", 7, 9, 0, 5), ("R", 12, 0), ("R", 2, 2), ("R", 2, 1), ("S", 2, 5, 1, 3), ("D", 2), ("G", 2, (0, 4)),
-    ("G", 2, (1, 3)), ("R", 6, 0), ("D", 6), ("R", 8, 0), ("D", 8), ("G", 8, (4, 1)), ("R", 7, 1), ("R", 12, 2),
-    ("S", 12, 5, 2, 2), ("R", 5, 0), ("S", 5, 10, 0, 5), ("R", 12, 1), ("D", 12), ("X", 2), ("X", 11),
-    ("G", 8, (2, 11)), ("G", 6, (1, 4)), ("R", 9, 2), ("X", 8), ("G", 12, (4, 8)), ("R", 9, 0), ("R", 7, 2),
-    ("D", 7), ("R", 10, 2), ("R", 10, 1), ("G", 7, (0, 1)), ("F", 0), ("X", 12), ("G", 7, (2, 12)), ("F", 12),
-    ("R", 9, 1), ("G", 9, (2, 11)), ("F", 2), ("R", 10, 0), ("R", 5, 2), ("R", 5, 1), ("D", 5), ("G", 5, (4, 3)),
-    ("G", 10, (4, 8)), ("F", 4), ("G", 3, (1,)), ("F", 1), ("G", 11, (3,)), ("F", 3), ("F", 11), ("X", 6),
-    ("G", 8, (6,)), ("F", 6), ("G", 5, (8,)), ("F", 8), ("X", 5), ("G", 7, (5,)), ("G", 9, (5,)), ("F", 9),
-    ("F", 5), ("X", 7), ("G", 10, (7,)), ("F", 10), ("F", 7),
+    ("S", 0, 2, 0, 0), ("S", 0, 9, 1, 1), ("S", 0, 3, 1, 2), ("S", 0, 6, 1, 3), ("S", 0, 4, 1, 4),
+    ("S", 0, 2, 2, 0), ("S", 0, 9, 0, 1), ("S", 0, 3, 0, 2), ("S", 0, 6, 2, 3), ("S", 0, 4, 2, 4), ("D", 0),
+    ("self", 0), ("X", 0), ("self", 1), ("S", 0, 9, 2, 1), ("S", 0, 3, 2, 2), ("S", 0, 6, 0, 3), ("R", 2, 0),
+    ("R", 9, 1), ("R", 3, 1), ("S", 3, 10, 1, 0), ("R", 6, 1), ("S", 6, 1, 1, 5), ("S", 0, 4, 0, 4), ("R", 4, 1),
+    ("S", 4, 5, 1, 4), ("R", 2, 2), ("S", 2, 10, 2, 2), ("R", 9, 0), ("R", 3, 0), ("S", 3, 10, 0, 0),
+    ("S", 3, 7, 0, 1), ("S", 9, 7, 1, 2), ("R", 6, 2), ("S", 6, 1, 2, 5), ("R", 4, 2), ("S", 4, 5, 2, 4),
+    ("R", 1, 1), ("R", 10, 1), ("S", 10, 2, 1, 3), ("S", 10, 12, 1, 0), ("R", 9, 2), ("D", 9), ("R", 3, 2),
+    ("S", 3, 7, 2, 1), ("D", 3), ("R", 6, 0), ("S", 6, 1, 0, 5), ("D", 6), ("R", 4, 0), ("S", 4, 5, 0, 4), ("D", 4),
+    ("G", 6, (0,)), ("G", 9, (0,)), ("G", 4, (0,)), ("X", 9), ("G", 3, (9,)), ("G", 6, (9,)), ("G", 4, (9,)),
+    ("R", 1, 2), ("S", 1, 8, 2, 5), ("R", 10, 0), ("R", 7, 0), ("S", 7, 12, 0, 1), ("R", 10, 2),
+    ("S", 10, 12, 2, 0), ("S", 2, 11, 2, 0), ("S", 9, 11, 0, 1), ("D", 10), ("R", 5, 1), ("S", 5, 8, 1, 3),
+    ("X", 6), ("X", 3), ("X", 4), ("G", 3, (6,)), ("G", 4, (3, 6)), ("G", 10, (6, 9, 4)), ("R", 2, 1),
+    ("G", 2, (4, 9)), ("R", 1, 0), ("S", 1, 8, 0, 5), ("D", 1), ("R", 12, 1), ("S", 12, 11, 1, 3), ("R", 7, 2),
+    ("R", 7, 1), ("D", 7), ("R", 5, 2), ("X", 10), ("G", 1, (3, 9, 4, 10)), ("G", 7, (4,)), ("X", 1),
+    ("G", 2, (1,)), ("G", 7, (1,)), ("F", 2), ("R", 8, 1), ("R", 8, 2), ("R", 12, 2), ("R", 12, 0), ("D", 12),
+    ("R", 5, 0), ("D", 5), ("X", 7), ("G", 5, (7, 10, 0, 9)), ("G", 12, (4, 1, 6)), ("F", 7), ("F", 0), ("F", 9),
+    ("F", 6), ("R", 8, 0), ("R", 11, 1), ("R", 11, 2), ("R", 11, 0), ("X", 12), ("X", 5), ("G", 5, (12,)),
+    ("G", 8, (3, 12, 10)), ("G", 11, (5, 4, 1)), ("F", 3), ("F", 12), ("F", 8), ("F", 10), ("F", 5), ("F", 4),
+    ("F", 11), ("F", 1),
 )
 
 
@@ -55,16 +55,22 @@
     return tuple((4 - v) % 4 for v in offset)
 
 
-def kernel(emb_ref, dest_ref, out_ref, blk, labc, racc, cacc, res,
+def kernel(emb_any, dest_any, out_ref, emb_ref, dest_ref, load_sem, blk, labc, racc, cacc, part, res,
            ici_send, ici_recv, d2d_send, d2d_recv, res_send, res_recv):
     chip, core = place()
     other = 1 - core
+    loads = [pltpu.make_async_copy(emb_any, emb_ref, load_sem.at[0]),
+             pltpu.make_async_copy(dest_any, dest_ref, load_sem.at[1])]
+    for load in loads:
+        load.start()
     barrier = pltpu.get_barrier_semaphore()
     for unit in UNITS:
         pl.semaphore_signal(barrier, inc=1, device_id=device(chip, unit, core), device_id_type=MESH)
     sibling = device(chip, (0, 0, 0), other)
     pl.semaphore_signal(barrier, inc=1, device_id=sibling, device_id_type=MESH)
 
+    for load in loads:
+        load.wait()
     values = emb_ref[...]
     sums = jnp.sum(values * values, axis=1, keepdims=True)
     blk[0, core, 0:HALF, :] = (values * lax.rsqrt(sums + 1e-06)).astype(jnp.bfloat16)
@@ -92,7 +98,7 @@
 
     def result(slot, half, sender):
         return pltpu.make_async_remote_copy(
-            src_ref=cacc.at[slot, half], dst_ref=res.at[slot, sender],
+            src_ref=part.at[slot, half], dst_ref=res.at[slot, sender],
             send_sem=res_send.at[slot, half], recv_sem=res_recv.at[slot, sender],
             device_id=device(chip, OFFSETS[slot], half), device_id_type=MESH)
 
@@ -162,7 +168,11 @@
             best = jnp.max(racc[slot].T.reshape(16, 8, HALF), axis=0)
             if slot in have_cacc:
                 best = jnp.maximum(best, cacc[slot, core])
-            cacc[slot, core] = best
+            part[slot, core] = jnp.max(best, axis=0, keepdims=True)
+        if slot in have_cacc:
+            part[slot, other] = jnp.max(cacc[slot, other], axis=0, keepdims=True)
+            if slot not in have_racc:
+                part[slot, core] = jnp.max(cacc[slot, core], axis=0, keepdims=True)
         if slot == 0:
             copy = result(0, other, 1)
             copy.start()
@@ -199,7 +209,7 @@
             finish(act[1])
 
     result(0, other, 1).wait_recv()
-    best = jnp.maximum(cacc[0, core], res[0, 1])
+    best = jnp.maximum(part[0, core], res[0, 1])
     for slot in range(1, SLOTS):
         if slot in have_cacc:
             for sender in range(2):
@@ -208,7 +218,7 @@
         else:
             result(slot, core, core).wait_recv()
             best = jnp.maximum(best, res[slot, core])
-    out_ref[...] = jnp.max(best, axis=0, keepdims=True)
+    out_ref[...] = best.reshape(HALF)
     for copy in sends:
         copy.wait_send()
 
@@ -216,15 +226,19 @@
 def on_device(embeddings, destinations):
     nearest = pl.pallas_call(
         kernel,
-        out_shape=jax.ShapeDtypeStruct((1, HALF), jnp.float32),
-        in_specs=[pl.BlockSpec(memory_space=pltpu.VMEM)] * 2,
+        out_shape=jax.ShapeDtypeStruct((HALF,), jnp.float32),
+        in_specs=[pl.BlockSpec(memory_space=pl.ANY)] * 2,
         out_specs=pl.BlockSpec(memory_space=pltpu.VMEM),
         scratch_shapes=[
+            pltpu.VMEM((HALF, WIDTH), jnp.float32),
+            pltpu.VMEM((1, HALF), jnp.int32),
+            pltpu.SemaphoreType.DMA((2,)),
             pltpu.VMEM((SLOTS, 2, HALF + TILE, WIDTH), jnp.bfloat16),
             pltpu.VMEM((SLOTS, HALF, 128), jnp.float32),
             pltpu.VMEM((SLOTS, HALF, 128), jnp.float32),
             pltpu.VMEM((SLOTS, 2, 8, HALF), jnp.float32),
-            pltpu.VMEM((SLOTS, 2, 8, HALF), jnp.float32),
+            pltpu.VMEM((SLOTS, 2, 1, HALF), jnp.float32),
+            pltpu.VMEM((SLOTS, 2, 1, HALF), jnp.float32),
             pltpu.SemaphoreType.DMA((SLOTS, len(PARTS))),
             pltpu.SemaphoreType.DMA((SLOTS, len(PARTS))),
             pltpu.SemaphoreType.DMA((SLOTS,)),
@@ -233,9 +247,9 @@
             pltpu.SemaphoreType.DMA((SLOTS, 2)),
         ],
         compiler_params=pltpu.CompilerParams(
-            collective_id=0, has_side_effects=True, vmem_limit_bytes=48 * 2**20),
+            collective_id=0, has_side_effects=True, vmem_limit_bytes=63 * 2**20),
     )(embeddings, destinations.reshape(1, HALF))
-    return nearest.reshape(HALF)
+    return nearest
 
 
 def solution(mesh):

time: 45.6 us -> 41.8 us (0.917)
  Pallas kernels: 43.1 us -> 40.4 us
  other arithmetic: 0.6 us -> 0 us
  local copies, waits for them, and re-layouts: 1.81 us -> 1.26 us
    pallas_call x1, Pallas kernels: 43.1 us -> 40.4 us  [on_device(): pl.pallas_call(kernel, out_shape=jax.ShapeDtypeStruct((HALF,), jnp.float3...]
    pallas_call x1 -> x0, other arithmetic: 0.6 us -> none  [on_device(): pl.pallas_call(kernel, out_shape=jax.ShapeDtypeStruct((1, HALF), jnp.floa...]
    unnamed x4 -> x1, local copies, waits for them, and re-layouts: 1.81 us -> 1.26 us
where the time goes in v2:
time: 41.8 us; the launch traced here: 41.7 us
  Pallas kernels  40.4 us (97%)
  local copies, waits for them, and re-layouts  1.26 us (3%)
    pallas_call x1, Pallas kernels, on_device(): pl.pallas_call(kernel, out_shape=jax.ShapeDtypeStruct((HALF,), jnp.float3...  40.4 us
    unnamed x1, local copies, waits for them, and re-layouts  1.26 us

profile of v2, /device:TPU:1, one launch (start us, length us, event | category | flops | bytes accessed | tf_op | source)
XLA Modules:
  0.0 41.7 jit_solution(4330464832883928521)
XLA Ops:
  0.0 40.4 %shard_map.28 = f32[384]{0:T(512)} custom-call(f32[384,512]{1,0:T(8,128)} %emb_any.1, s32[1,384]{1,0:T(1,128)} %bitcast.1), custom_call_target="tpu_custom_call" | custom-call | tf_op jit(solution)/shard_map/pallas_call | solution.py:227
  40.4 1.3 %copy.4 = f32[384]{0:T(512)} copy(f32[384]{0:T(512)} %shard_map.28) | data formatting | bytes 3072

commit v3 on v2

v3 whole, which is shorter than its diff:
```python
import functools

import jax
import jax.numpy as jnp
from jax import lax
from jax.experimental import pallas as pl
from jax.experimental.pallas import tpu as pltpu
from jax.sharding import PartitionSpec as P

MESH = pl.DeviceIdType.MESH
HALF = 384
WIDTH = 512
TILE = 16
UNITS = ((1, 0, 0), (3, 0, 0), (0, 1, 0), (0, 3, 0), (0, 0, 1), (0, 0, 3))
SLOTS = 13
OFFSETS = ((0, 0, 0), (0, 1, 0), (1, 1, 0), (0, 3, 0), (1, 0, 0), (3, 0, 0), (3, 0, 3), (0, 2, 0), (3, 0, 2), (0, 0, 1), (1, 2, 0), (1, 3, 0), (0, 0, 2))
PARTS = ((0, 128), (128, 128), (256, 144))
ACTS = (
    ("S", 0, 4, 0, 0), ("S", 0, 5, 0, 1), ("S", 0, 1, 2, 2), ("S", 0, 3, 2, 3), ("S", 0, 9, 0, 4), ("D", 0),
    ("self", 0), ("X", 0), ("self", 1), ("S", 0, 4, 1, 0), ("S", 0, 5, 1, 1), ("S", 0, 1, 1, 2), ("S", 0, 3, 1, 3),
    ("S", 0, 9, 2, 4), ("S", 0, 5, 2, 1), ("S", 0, 3, 0, 3), ("S", 0, 9, 1, 4), ("R", 4, 0), ("S", 4, 2, 0, 2),
    ("R", 5, 0), ("S", 5, 6, 0, 5), ("R", 1, 2), ("S", 1, 2, 2, 0), ("R", 3, 2), ("R", 9, 0), ("S", 0, 4, 2, 0),
    ("R", 4, 1), ("S", 4, 2, 1, 2), ("S", 4, 11, 1, 3), ("R", 5, 1), ("S", 5, 6, 1, 5), ("R", 1, 1), ("R", 3, 1),
    ("R", 9, 2), ("S", 9, 12, 2, 4), ("S", 3, 11, 2, 0), ("S", 4, 11, 0, 3), ("R", 6, 0), ("R", 2, 2), ("R", 5, 2),
    ("S", 5, 6, 2, 5), ("D", 5), ("R", 2, 0), ("S", 2, 1, 0, 1), ("S", 2, 10, 0, 2), ("R", 3, 0), ("D", 3),
    ("R", 9, 1), ("S", 9, 12, 1, 4), ("D", 9), ("G", 9, (0,)), ("G", 3, (0,)), ("G", 5, (0,)), ("F", 0),
    ("S", 6, 8, 0, 5), ("S", 2, 10, 2, 2), ("S", 9, 12, 0, 4), ("X", 3), ("X", 5), ("G", 9, (3, 5)), ("G", 5, (3,)),
    ("R", 6, 1), ("R", 4, 2), ("D", 4), ("R", 2, 1), ("D", 2), ("R", 11, 1), ("S", 11, 10, 1, 3), ("R", 12, 2),
    ("S", 12, 8, 2, 1), ("X", 9), ("G", 2, (5, 3, 9)), ("G", 4, (9, 5, 3)), ("S", 6, 8, 1, 5), ("S", 1, 7, 1, 2),
    ("S", 3, 7, 2, 3), ("R", 6, 2), ("D", 6), ("R", 1, 0), ("X", 2), ("X", 4), ("G", 6, (2, 3, 4)),
    ("G", 1, (3, 9)), ("R", 11, 2), ("R", 10, 0), ("S", 10, 7, 0, 1), ("R", 11, 0), ("D", 11), ("R", 12, 1),
    ("X", 6), ("G", 11, (9,)), ("G", 1, (6,)), ("G", 9, (6,)), ("F", 1), ("R", 8, 0), ("R", 8, 2), ("R", 10, 2),
    ("R", 10, 1), ("D", 10), ("R", 12, 0), ("D", 12), ("X", 11), ("G", 12, (3, 11, 2)), ("G", 10, (9, 6, 5)),
    ("G", 6, (11,)), ("F", 11), ("F", 3), ("R", 8, 1), ("X", 10), ("X", 12), ("G", 8, (2, 10, 4, 5)),
    ("G", 10, (12,)), ("F", 10), ("F", 8), ("F", 2), ("F", 4), ("F", 5), ("R", 7, 1), ("R", 7, 2), ("R", 7, 0),
    ("G", 7, (9, 6, 12)), ("F", 6), ("F", 7), ("F", 12), ("F", 9),
)


def place():
    cluster = lax.axis_index("cluster")
    group = lax.axis_index("group")
    core = lax.rem(cluster, 2)
    z = cluster // 2 + 2 * lax.rem(group // 4, 2)
    return (lax.rem(group, 4), group // 8, z), core


def device(chip, offset, core):
    x, y, z = (lax.rem(a + b, 4) for a, b in zip(chip, offset))
    return (lax.rem(z, 2) * 2 + core, (y * 2 + z // 2) * 4 + x)


def back(offset):
    return tuple((4 - v) % 4 for v in offset)


def kernel(emb_any, dest_any, out_ref, emb_ref, dest_ref, load_sem, blk, labc, racc, cacc, part, res,
           ici_send, ici_recv, d2d_send, d2d_recv, res_send, res_recv):
    chip, core = place()
    other = 1 - core
    barrier = pltpu.get_barrier_semaphore()
    for unit in UNITS:
        pl.semaphore_signal(barrier, inc=1, device_id=device(chip, unit, core), device_id_type=MESH)
    sibling = device(chip, (0, 0, 0), other)
    pl.semaphore_signal(barrier, inc=1, device_id=sibling, device_id_type=MESH)

    loads = [pltpu.make_async_copy(emb_any, emb_ref, load_sem.at[0]),
             pltpu.make_async_copy(dest_any, dest_ref, load_sem.at[1])]
    for load in loads:
        load.start()
    for load in loads:
        load.wait()
    values = emb_ref[...]
    sums = jnp.sum(values * values, axis=1, keepdims=True)
    blk[0, core, 0:HALF, :] = (values * lax.rsqrt(sums + 1e-06)).astype(jnp.bfloat16)
    label = (dest_ref[...] // 32).astype(jnp.float32)
    tile = jnp.concatenate(
        [jnp.broadcast_to(label, (TILE, HALF)), jnp.zeros((TILE, WIDTH - HALF), jnp.float32)], axis=1)
    blk[0, core, HALF:HALF + TILE, :] = tile.astype(jnp.bfloat16)
    pl.semaphore_wait(barrier, len(UNITS) + 1)

    def ici(src, dst, piece, e):
        first, count = PARTS[piece]
        rows = pl.ds(first, count)
        return pltpu.make_async_remote_copy(
            src_ref=blk.at[src, core, rows], dst_ref=blk.at[dst, core, rows],
            send_sem=ici_send.at[0], recv_sem=ici_recv.at[dst, piece],
            device_id=device(chip, back(UNITS[e]), core), device_id_type=MESH)

    def d2d(slot, half):
        return pltpu.make_async_remote_copy(
            src_ref=blk.at[slot, half], dst_ref=blk.at[slot, half],
            send_sem=d2d_send.at[0], recv_sem=d2d_recv.at[slot],
            device_id=sibling, device_id_type=MESH)

    def result(slot, half, sender):
        return pltpu.make_async_remote_copy(
            src_ref=part.at[2 * slot + half], dst_ref=res.at[2 * slot + sender],
            send_sem=res_send.at[0], recv_sem=res_recv.at[0],
            device_id=device(chip, OFFSETS[slot], half), device_id_type=MESH)

    def results(count):
        return pltpu.make_async_remote_copy(
            src_ref=part.at[pl.ds(0, count)], dst_ref=res.at[pl.ds(0, count)],
            send_sem=res_send.at[0], recv_sem=res_recv.at[0],
            device_id=sibling, device_id_type=MESH)

    def sent(first, count, sem):
        rows = blk.at[pl.ds(first, count), core]
        return pltpu.make_async_remote_copy(
            src_ref=rows, dst_ref=rows, send_sem=sem, recv_sem=ici_recv.at[0, 0],
            device_id=sibling, device_id_type=MESH)

    def labels(slot, half):
        return blk[slot, half, HALF:HALF + TILE, :].astype(jnp.float32)[0:8, 0:HALF]

    def column_labels(slot):
        row = labels(slot, core)
        labc[slot] = jnp.concatenate([row] * 16, axis=0).T

    have_labc, have_racc, have_cacc = set(), set(), set()

    def prepare(slot):
        if slot not in have_labc:
            have_labc.add(slot)
            column_labels(slot)

    def masked(scores, own, row):
        count = scores.shape[0] // 8
        match = own.reshape(count, 8, 128) == row[None]
        return jnp.where(match, scores.reshape(count, 8, 128), jnp.float32(-2.0))

    def dot(lhs, rhs):
        return lax.dot_general(lhs, rhs, (((1,), (1,)), ((), ())), preferred_element_type=jnp.float32)

    def own_block(which):
        prepare(0)
        half = core if which == 0 else other
        scores = dot(blk[0, core, 0:HALF, :], blk[0, half, 0:HALF, :])
        row = labels(0, half)
        own = labc[0]
        best = racc[0] if 0 in have_racc else jnp.full((HALF, 128), -2.0, jnp.float32)
        for q in range(0, HALF, 128):
            t = masked(scores[:, q:q + 128], own, row[:, q:q + 128]).reshape(HALF, 128)
            if which == 0:
                i = lax.broadcasted_iota(jnp.int32, (HALF, 128), 0)
                j = lax.broadcasted_iota(jnp.int32, (HALF, 128), 1) + q
                t = jnp.where(i == j, jnp.float32(-2.0), t)
            best = jnp.maximum(best, t)
        racc[0] = best
        have_racc.add(0)

    def pairs(slot, others):
        prepare(slot)
        lhs = blk[slot, core, 0:HALF, :]
        own = labc[slot]
        best = racc[slot] if slot in have_racc else None
        for mate in others:
            scores = dot(lhs, blk[mate, :, 0:HALF, :].reshape(2 * HALF, WIDTH))
            for half in range(2):
                row = labels(mate, half)
                for q in range(0, HALF, 128):
                    at = half * HALF + q
                    t = masked(scores[:, at:at + 128], own, row[:, q:q + 128])
                    top = jnp.max(t, axis=0)
                    if mate in have_cacc:
                        top = jnp.maximum(top, cacc[mate, half, :, q:q + 128])
                    cacc[mate, half, :, q:q + 128] = top
                    t = t.reshape(HALF, 128)
                    best = t if best is None else jnp.maximum(best, t)
            have_cacc.add(mate)
        racc[slot] = best
        have_racc.add(slot)

    def finish(slot):
        if slot in have_racc:
            best = jnp.max(racc[slot].T.reshape(16, 8, HALF), axis=0)
            if slot in have_cacc:
                best = jnp.maximum(best, cacc[slot, core])
            part[2 * slot + core] = jnp.max(best, axis=0, keepdims=True)
        if slot in have_cacc:
            part[2 * slot + other] = jnp.max(cacc[slot, other], axis=0, keepdims=True)
            if slot not in have_racc:
                part[2 * slot + core] = jnp.max(cacc[slot, core], axis=0, keepdims=True)

    def send_back(slot):
        halves = (other,) if slot == 0 else (0, 1) if slot in have_cacc else (core,)
        for half in halves:
            result(slot, half, 1 if slot == 0 else core).start()

    finished = []
    for act in ACTS + (("",),):
        kind = act[0]
        if kind != "F":
            for slot in finished:
                send_back(slot)
            finished = []
        if kind == "S":
            ici(act[1], act[2], act[3], act[4]).start()
        elif kind == "R":
            ici(act[1], act[1], act[2], 0).wait_recv()
        elif kind == "D":
            d2d(act[1], core).start()
        elif kind == "X":
            d2d(act[1], other).wait_recv()
        elif kind == "self":
            own_block(act[1])
        elif kind == "G":
            pairs(act[1], act[2])
        elif kind == "F":
            finish(act[1])
            finished.append(act[1])

    sent(1, SLOTS - 1, ici_send.at[0]).wait_send()
    sent(0, sum(act[0] == "D" for act in ACTS), d2d_send.at[0]).wait_send()
    count = 1 + sum(2 if slot in have_cacc else 1 for slot in range(1, SLOTS))
    results(count).wait_send()
    results(count).wait_recv()
    best = jnp.maximum(part[core], res[1])
    for slot in range(1, SLOTS):
        if slot in have_cacc:
            best = jnp.maximum(best, jnp.maximum(res[2 * slot], res[2 * slot + 1]))
        else:
            best = jnp.maximum(best, res[2 * slot + core])
    out_ref[...] = best.reshape(HALF)


def on_device(embeddings, destinations):
    nearest = pl.pallas_call(
        kernel,
        out_shape=jax.ShapeDtypeStruct((HALF,), jnp.float32),
        in_specs=[pl.BlockSpec(memory_space=pl.ANY)] * 2,
        out_specs=pl.BlockSpec(memory_space=pltpu.VMEM),
        scratch_shapes=[
            pltpu.VMEM((HALF, WIDTH), jnp.float32),
            pltpu.VMEM((1, HALF), jnp.int32),
            pltpu.SemaphoreType.DMA((2,)),
            pltpu.VMEM((SLOTS, 2, HALF + TILE, WIDTH), jnp.bfloat16),
            pltpu.VMEM((SLOTS, HALF, 128), jnp.float32),
            pltpu.VMEM((SLOTS, HALF, 128), jnp.float32),
            pltpu.VMEM((SLOTS, 2, 8, HALF), jnp.float32),
            pltpu.VMEM((2 * SLOTS, 1, HALF), jnp.float32),
            pltpu.VMEM((2 * SLOTS, 1, HALF), jnp.float32),
            pltpu.SemaphoreType.DMA((1,)),
            pltpu.SemaphoreType.DMA((SLOTS, len(PARTS))),
            pltpu.SemaphoreType.DMA((1,)),
            pltpu.SemaphoreType.DMA((SLOTS,)),
            pltpu.SemaphoreType.DMA((1,)),
            pltpu.SemaphoreType.DMA((1,)),
        ],
        compiler_params=pltpu.CompilerParams(
            collective_id=0, has_side_effects=True, vmem_limit_bytes=63 * 2**20),
    )(embeddings, destinations.reshape(1, HALF))
    return nearest


def solution(mesh):
    spec = P(("cluster", "group"), None)
    return jax.shard_map(
        on_device, mesh=mesh, in_specs=(spec, spec), out_specs=P(("cluster", "group")), check_vma=False
    )
```

time: 41.8 us -> 39.9 us (0.955)
  Pallas kernels: 40.4 us -> 38.5 us
    pallas_call x1, Pallas kernels: 40.4 us -> 38.5 us  [on_device(): pl.pallas_call(kernel, out_shape=jax.ShapeDtypeStruct((HALF,), jnp.float3...]
where the time goes in v3:
time: 39.9 us; the launch traced here: 39.8 us
  Pallas kernels  38.5 us (96%)
  local copies, waits for them, and re-layouts  1.26 us (3%)
    pallas_call x1, Pallas kernels, on_device(): pl.pallas_call(kernel, out_shape=jax.ShapeDtypeStruct((HALF,), jnp.float3...  38.5 us
    unnamed x1, local copies, waits for them, and re-layouts  1.26 us

profile of v3, /device:TPU:1, one launch (start us, length us, event | category | flops | bytes accessed | tf_op | source)
XLA Modules:
  0.0 39.8 jit_solution(4178106495334777095)
XLA Ops:
  0.0 38.5 %shard_map.28 = f32[384]{0:T(512)} custom-call(f32[384,512]{1,0:T(8,128)} %emb_any.1, s32[1,384]{1,0:T(1,128)} %bitcast.1), custom_call_target="tpu_custom_call" | custom-call | tf_op jit(solution)/shard_map/pallas_call | solution.py:229
  38.5 1.3 %copy.4 = f32[384]{0:T(512)} copy(f32[384]{0:T(512)} %shard_map.28) | data formatting | bytes 3072

commit v4 on v3

--- a/solution.py
+++ b/solution.py
@@ -23,17 +23,17 @@
     ("R", 4, 1), ("S", 4, 2, 1, 2), ("S", 4, 11, 1, 3), ("R", 5, 1), ("S", 5, 6, 1, 5), ("R", 1, 1), ("R", 3, 1),
     ("R", 9, 2), ("S", 9, 12, 2, 4), ("S", 3, 11, 2, 0), ("S", 4, 11, 0, 3), ("R", 6, 0), ("R", 2, 2), ("R", 5, 2),
     ("S", 5, 6, 2, 5), ("D", 5), ("R", 2, 0), ("S", 2, 1, 0, 1), ("S", 2, 10, 0, 2), ("R", 3, 0), ("D", 3),
-    ("R", 9, 1), ("S", 9, 12, 1, 4), ("D", 9), ("G", 9, (0,)), ("G", 3, (0,)), ("G", 5, (0,)), ("F", 0),
-    ("S", 6, 8, 0, 5), ("S", 2, 10, 2, 2), ("S", 9, 12, 0, 4), ("X", 3), ("X", 5), ("G", 9, (3, 5)), ("G", 5, (3,)),
-    ("R", 6, 1), ("R", 4, 2), ("D", 4), ("R", 2, 1), ("D", 2), ("R", 11, 1), ("S", 11, 10, 1, 3), ("R", 12, 2),
-    ("S", 12, 8, 2, 1), ("X", 9), ("G", 2, (5, 3, 9)), ("G", 4, (9, 5, 3)), ("S", 6, 8, 1, 5), ("S", 1, 7, 1, 2),
-    ("S", 3, 7, 2, 3), ("R", 6, 2), ("D", 6), ("R", 1, 0), ("X", 2), ("X", 4), ("G", 6, (2, 3, 4)),
-    ("G", 1, (3, 9)), ("R", 11, 2), ("R", 10, 0), ("S", 10, 7, 0, 1), ("R", 11, 0), ("D", 11), ("R", 12, 1),
-    ("X", 6), ("G", 11, (9,)), ("G", 1, (6,)), ("G", 9, (6,)), ("F", 1), ("R", 8, 0), ("R", 8, 2), ("R", 10, 2),
-    ("R", 10, 1), ("D", 10), ("R", 12, 0), ("D", 12), ("X", 11), ("G", 12, (3, 11, 2)), ("G", 10, (9, 6, 5)),
-    ("G", 6, (11,)), ("F", 11), ("F", 3), ("R", 8, 1), ("X", 10), ("X", 12), ("G", 8, (2, 10, 4, 5)),
-    ("G", 10, (12,)), ("F", 10), ("F", 8), ("F", 2), ("F", 4), ("F", 5), ("R", 7, 1), ("R", 7, 2), ("R", 7, 0),
-    ("G", 7, (9, 6, 12)), ("F", 6), ("F", 7), ("F", 12), ("F", 9),
+    ("R", 9, 1), ("S", 9, 12, 1, 4), ("D", 9), ("G", 5, (0,)), ("G", 3, (0,)), ("G", 9, (0,)), ("X", 5),
+    ("G", 3, (5,)), ("S", 6, 8, 0, 5), ("X", 3), ("X", 9), ("G", 9, (3,)), ("G", 5, (9,)), ("S", 2, 10, 2, 2),
+    ("S", 9, 12, 0, 4), ("R", 6, 1), ("R", 4, 2), ("D", 4), ("R", 2, 1), ("D", 2), ("R", 11, 1),
+    ("S", 11, 10, 1, 3), ("R", 12, 2), ("S", 12, 8, 2, 1), ("G", 2, (5, 3, 9)), ("G", 4, (5, 3, 9)),
+    ("S", 6, 8, 1, 5), ("S", 1, 7, 1, 2), ("S", 3, 7, 2, 3), ("R", 6, 2), ("D", 6), ("R", 1, 0), ("X", 4), ("X", 2),
+    ("G", 6, (3, 4, 9, 2)), ("G", 1, (9, 3)), ("R", 11, 2), ("R", 10, 0), ("S", 10, 7, 0, 1), ("R", 11, 0),
+    ("D", 11), ("R", 12, 1), ("X", 6), ("G", 11, (6, 9)), ("G", 1, (6,)), ("F", 1), ("R", 8, 0), ("R", 8, 2),
+    ("R", 10, 2), ("R", 10, 1), ("D", 10), ("R", 12, 0), ("D", 12), ("X", 11), ("G", 12, (0, 11, 2, 3)),
+    ("G", 10, (9, 5, 6)), ("F", 0), ("F", 11), ("F", 3), ("F", 5), ("R", 8, 1), ("R", 7, 1), ("R", 7, 2), ("X", 10),
+    ("G", 12, (10,)), ("G", 8, (10, 4, 2)), ("F", 10), ("F", 4), ("F", 8), ("F", 2), ("R", 7, 0), ("X", 12),
+    ("G", 7, (6, 12, 9)), ("F", 6), ("F", 12), ("F", 7), ("F", 9),
 )
 
 

time: 39.9 us -> 39.6 us (level)
  no operation moved by 1% of the time
where the time goes in v4:
time: 39.6 us; the launch traced here: 39.4 us
  Pallas kernels  38.2 us (96%)
  local copies, waits for them, and re-layouts  1.26 us (3%)
    pallas_call x1, Pallas kernels, on_device(): pl.pallas_call(kernel, out_shape=jax.ShapeDtypeStruct((HALF,), jnp.float3...  38.2 us
    unnamed x1, local copies, waits for them, and re-layouts  1.26 us

profile of v4, /device:TPU:1, one launch (start us, length us, event | category | flops | bytes accessed | tf_op | source)
XLA Modules:
  0.0 39.4 jit_solution(14003211550390120037)
XLA Ops:
  0.0 38.2 %shard_map.28 = f32[384]{0:T(512)} custom-call(f32[384,512]{1,0:T(8,128)} %emb_any.1, s32[1,384]{1,0:T(1,128)} %bitcast.1), custom_call_target="tpu_custom_call" | custom-call | tf_op jit(solution)/shard_map/pallas_call | solution.py:229
  38.2 1.3 %copy.4 = f32[384]{0:T(512)} copy(f32[384]{0:T(512)} %shard_map.28) | data formatting | bytes 3072

commit v5 on v4

--- a/solution.py
+++ b/solution.py
@@ -54,6 +54,10 @@
     return tuple((4 - v) % 4 for v in offset)
 
 
+def hops(slot):
+    return sum(min(v, 4 - v) for v in OFFSETS[slot])
+
+
 def kernel(emb_any, dest_any, out_ref, emb_ref, dest_ref, load_sem, blk, labc, racc, cacc, part, res,
            ici_send, ici_recv, d2d_send, d2d_recv, res_send, res_recv):
     chip, core = place()
@@ -192,7 +196,7 @@
     for act in ACTS + (("",),):
         kind = act[0]
         if kind != "F":
-            for slot in finished:
+            for slot in sorted(finished, key=hops, reverse=True):
                 send_back(slot)
             finished = []
         if kind == "S":

time: 39.6 us -> 39.6 us (level)
  no operation moved by 1% of the time
where the time goes in v5:
time: 39.6 us; the launch traced here: 39.4 us
  Pallas kernels  38.2 us (96%)
  local copies, waits for them, and re-layouts  1.26 us (3%)
    pallas_call x1, Pallas kernels, on_device(): pl.pallas_call(kernel, out_shape=jax.ShapeDtypeStruct((HALF,), jnp.float3...  38.2 us
    unnamed x1, local copies, waits for them, and re-layouts  1.26 us

profile of v5, /device:TPU:1, one launch (start us, length us, event | category | flops | bytes accessed | tf_op | source)
XLA Modules:
  0.0 39.4 jit_solution(5970911565995504384)
XLA Ops:
  0.0 38.2 %shard_map.28 = f32[384]{0:T(512)} custom-call(f32[384,512]{1,0:T(8,128)} %emb_any.1, s32[1,384]{1,0:T(1,128)} %bitcast.1), custom_call_target="tpu_custom_call" | custom-call | tf_op jit(solution)/shard_map/pallas_call | solution.py:233
  38.2 1.3 %copy.4 = f32[384]{0:T(512)} copy(f32[384]{0:T(512)} %shard_map.28) | data formatting | bytes 3072
